TPU v7x, 32 devices: a whole 2x2x4 slice. The times are simulated.
32 devices in a mesh: clips: 2 (over x), rows: 16 (over z, y, core).
Axes of the slice: x: 2, y: 2, z: 4, core: 2. Of those that a mesh axis runs over, the one named last changes fastest.
Arguments:
- state_start: bfloat16 [1024, 128, 128], P(('clips', 'rows')), parts along dimension 0, may hold values from -6 to 6
- features: bfloat16 [2, 1024, 128, 128], P(None, ('clips', 'rows')), parts along dimension 1, may hold values from -6 to 6
- row_moves: int32 [2, 2048], P(None, ('clips', 'rows')), parts along dimension 1, may hold values from -4 to 4, as said below
- col_moves: int32 [2, 2048], P(None, ('clips', 'rows')), parts along dimension 1, may hold values from -4 to 4
- merging_weight: bfloat16 [3, 3, 256, 128], replicated, may hold values from -0.125 to 0.125
- first_weight: bfloat16 [3, 3, 128, 128], replicated, may hold values from -0.1875 to 0.1875
- second_weight: bfloat16 [3, 3, 128, 128], replicated, may hold values from -0.1875 to 0.1875
Outputs:
- states: bfloat16 [2, 1024, 128, 128], P(None, ('clips', 'rows')), parts along dimension 1
There are 2 independent parts, one for each index of `clips`. A program takes and returns all parts, laid end to end along the dimension named above; an argument that names none is the same for every part. Nothing has to cross between parts.
Inputs may be any that keep to these rules, and one draw needn't show every extreme that they name: `row_moves`: every source block lies on the destination block's own device or on the device just above or below it; in each frame, among the 64 destination blocks of one device at most 32 take their source from the device above and at most 32 from the device below, and some device takes exactly 32 from the device above and some device exactly 32 from the one below.
All inputs are finite; a program needn't handle non-finite values.
Results may differ from a plain program's by a relative error of at most 0.009.
Values may be sent and summed in bfloat16 or wider, within the bound.
A program may use at most 64 MiB of HBM per device.

v0:
```python
import functools

import jax
import jax.numpy as jnp
from jax import lax
from jax.experimental import pallas as pl
from jax.experimental.pallas import tpu as pltpu
from jax.sharding import PartitionSpec as P

BLOCK = 8
MESH = pl.DeviceIdType.MESH
F32 = jnp.float32
BF16 = jnp.bfloat16


def put_taps(dst, row, values, rows):
    cols, chan = dst.shape[1], dst.shape[2] // 3
    length = rows * cols
    col = lax.rem(lax.broadcasted_iota(jnp.int32, (length, chan), 0), cols)
    left = jnp.where(col == 0, 0.0, pltpu.roll(values, 1, 0))
    right = jnp.where(col == cols - 1, 0.0, pltpu.roll(values, length - 1, 0))
    for e, part in enumerate((left, values, right)):
        dst[pl.ds(row, rows), :, e * chan : (e + 1) * chan] = part.astype(BF16).reshape(rows, cols, chan)


def conv_pairs(src, pair, count, weight):
    cols, depth = src.shape[1], src.shape[2]
    rows = src[pl.ds(2 * pair, 2 * count + 2)].reshape(count + 1, 2, cols, depth)
    window = jnp.concatenate([rows[:count, 0], rows[:count, 1], rows[1:, 0], rows[1:, 1]], axis=-1)
    return jnp.dot(window.reshape(count * cols, 4 * depth), weight[...], preferred_element_type=F32)


def unpair(values, count, cols):
    chan = values.shape[1] // 2
    even = values[:, :chan].reshape(count, cols, chan)
    odd = values[:, chan:].reshape(count, cols, chan)
    return jnp.stack([even, odd], axis=1).reshape(2 * count * cols, chan)


def kernel(
    group, picks, lists, state, features, w_merge, w_first, w_second, out,
    st, ft, wm, w1, w2, own, pool, packed, xf, xw, xm, xd, acc, wp, ob,
    big_f, big_w, big_1, big_2, want_v, want, halo_f, halo_w,
    load_sem, want_sem, out_sem, send_sem, recv_sem,
):
    frames, rows, cols, chan = features.shape
    band, across = rows // BLOCK, cols // BLOCK
    blocks = band * across
    slots = blocks // 2
    area = BLOCK * BLOCK
    me = lax.axis_index("rows")
    has = (me > 0, me < group - 1)
    peer = (me - 1, me + 1)

    loads = [
        pltpu.make_async_copy(a, b, load_sem.at[i])
        for i, (a, b) in enumerate(((state, st), (features, ft), (w_merge, wm), (w_first, w1), (w_second, w2)))
    ]
    for load in loads:
        load.start()

    barrier = pltpu.get_barrier_semaphore()
    for side in (0, 1):
        @pl.when(has[side])
        def _():
            pl.semaphore_signal(barrier, inc=1, device_id={"rows": peer[side]}, device_id_type=MESH)
    pl.semaphore_wait(barrier, has[0].astype(jnp.int32) + has[1].astype(jnp.int32))

    def remote(kind, side, src, dst):
        return pltpu.make_async_remote_copy(
            src_ref=src, dst_ref=dst,
            send_sem=send_sem.at[kind, side], recv_sem=recv_sem.at[kind, 1 - side],
            device_id={"rows": peer[side]}, device_id_type=MESH,
        )

    def list_copy(side):
        return remote(0, side, lists.at[side], want_v.at[1 - side])

    def feature_copy(side):
        edge = pl.ds(0, 3) if side == 0 else pl.ds(rows - 3, 3)
        return remote(1, side, features.at[:, edge], halo_f.at[1 - side])

    def pack_copy(f, side):
        return remote(2 + f, side, packed.at[f, side], pool[f].at[pl.ds(blocks + (1 - side) * slots, slots)])

    def halo_copy(f, side):
        edge = pl.ds(0, 3) if side == 0 else pl.ds(rows - 3, 3)
        return remote(2 + frames + f, side, wp.at[f, edge], halo_w.at[f, 1 - side])

    def each_side(action):
        for side in (0, 1):
            @pl.when(has[side])
            def _():
                action(side)

    def arrived(copy_of, side):
        copy_of(1 - side).wait_recv()

    each_side(lambda side: list_copy(side).start())
    each_side(lambda side: feature_copy(side).start())

    def to_blocks(f, b, q, strip):
        for h in (0, 1):
            block = strip[:, h * BLOCK : (h + 1) * BLOCK].reshape(area, chan).astype(BF16)
            own[f][b * across + 2 * q + h] = block
            pool[f][b * across + 2 * q + h] = block

    loads[0].wait()

    def cut_body(i, carry):
        b, q = i // (across // 2), i % (across // 2)
        strip = st[pl.ds(b * BLOCK, BLOCK), pl.ds(pl.multiple_of(q * 2 * BLOCK, 2 * BLOCK), 2 * BLOCK), :]
        to_blocks(0, b, q, strip.astype(F32))
        return carry

    lax.fori_loop(0, blocks // 2, cut_body, 0)

    for side in (0, 1):
        @pl.when(has[side])
        def _():
            arrived(list_copy, side)
            fetch = pltpu.make_async_copy(want_v.at[side], want.at[side], want_sem.at[side])
            fetch.start()
            fetch.wait()

    def pack_and_send(f):
        def action(side):
            def body(k, carry):
                for u in range(4):
                    packed[f, side, 4 * k + u] = own[f][want[side, f, 4 * k + u]]
                return carry
            lax.fori_loop(0, slots // 4, body, 0)
            pack_copy(f, side).start()
        each_side(action)

    pack_and_send(0)

    for load in loads[2:]:
        load.wait()

    def widen(big, raw, first):
        for t in range(4):
            for e in range(3):
                spot = pl.ds((t * 3 + e) * chan, chan)
                for r in (0, 1):
                    lanes = slice(r * chan, (r + 1) * chan)
                    if 0 <= t - r <= 2:
                        big[spot, lanes] = raw[t - r, e, first : first + chan, :]
                    else:
                        big[spot, lanes] = jnp.zeros((chan, chan), BF16)

    widen(big_f, wm, 0)
    widen(big_w, wm, chan)
    widen(big_1, w1, 0)
    widen(big_2, w2, 0)

    loads[1].wait()

    def fill_taps(dst, src, offset, total, step):
        def body(i, carry):
            values = src[pl.ds(i * step, step)].astype(F32).reshape(step * cols, chan)
            put_taps(dst, offset + i * step, values, step)
            return carry
        lax.fori_loop(0, total // step, body, 0)

    def edge_rows(dst, buffer, side):
        start = 0 if side == 0 else rows + 3
        values = buffer[...].astype(F32).reshape(3 * cols, chan)
        put_taps(dst, start, values, 3)

    def edge_zero(dst, start, count):
        dst[pl.ds(start, count)] = jnp.zeros((count,) + dst.shape[1:], BF16)

    for f in range(frames):
        fill_taps(xf.at[f], ft.at[f], 3, rows, 4)
    for side in (0, 1):
        @pl.when(has[side])
        def _():
            arrived(feature_copy, side)
            for f in range(frames):
                edge_rows(xf.at[f], halo_f.at[side, f], side)

        @pl.when(jnp.logical_not(has[side]))
        def _():
            for f in range(frames):
                edge_zero(xf.at[f], 0 if side == 0 else rows + 3, 3)
            edge_zero(xw, 0 if side == 0 else rows + 3, 3)

    pairs = rows // 2
    for f in range(frames):
        def feature_body(i, carry):
            count = (pairs + 2) // 3
            acc[f, pl.ds(i * count, count)] = conv_pairs(xf.at[f], i * count, count, big_f).reshape(count, cols, 2 * chan)
            return carry
        lax.fori_loop(0, 3, feature_body, 0)

    def merge_pairs(f, pair, count):
        total = acc[f, pl.ds(pair, count)].reshape(count * cols, 2 * chan) + conv_pairs(xw, pair, count, big_w)
        total = jnp.maximum(total, 0.1 * total)
        put_taps(xm, 2 * pair, unpair(total, count, cols), 2 * count)

    for f in range(frames):
        each_side(lambda side: arrived(functools.partial(pack_copy, f), side))

        def gather_body(i, carry):
            b, q = i // (across // 2), i % (across // 2)
            halves = [
                pool[f][picks[f, b * across + 2 * q + h]].astype(F32).reshape(BLOCK, BLOCK, chan) for h in (0, 1)
            ]
            strip = jnp.concatenate(halves, axis=1).astype(BF16)
            wp[f, pl.ds(b * BLOCK, BLOCK), pl.ds(pl.multiple_of(q * 2 * BLOCK, 2 * BLOCK), 2 * BLOCK), :] = strip
            return carry

        half = across // 2
        lax.fori_loop(0, half, gather_body, 0)
        lax.fori_loop((band - 1) * half, band * half, gather_body, 0)
        each_side(lambda side: halo_copy(f, side).start())
        lax.fori_loop(half, (band - 1) * half, gather_body, 0)
        fill_taps(xw, wp.at[f], 3, rows, 4)

        inner = (pairs - 2) // 2
        lax.fori_loop(0, 2, lambda i, c: (merge_pairs(f, 2 + i * inner, inner), c)[1], 0)
        for side in (0, 1):
            @pl.when(has[side])
            def _():
                arrived(functools.partial(halo_copy, f), side)
                edge_rows(xw, halo_w.at[f, side], side)
            merge_pairs(f, 0 if side == 0 else pairs, 2)

            @pl.when(jnp.logical_not(has[side]))
            def _():
                edge_zero(xm, 0 if side == 0 else rows + 2, 2)

        count = (pairs + 1 + 2) // 3

        def middle_body(i, carry):
            pair = jnp.minimum(i * count, pairs + 1 - count)
            total = jnp.maximum(conv_pairs(xm, pair, count, big_1), 0.0)
            put_taps(xd, 2 * pair, unpair(total, count, cols), 2 * count)
            return carry

        lax.fori_loop(0, 3, middle_body, 0)
        for side in (0, 1):
            @pl.when(jnp.logical_not(has[side]))
            def _():
                edge_zero(xd, 0 if side == 0 else rows + 1, 1)

        per = BLOCK // 2

        def last_body(b, carry):
            total = unpair(conv_pairs(xd, b * per, per, big_2), per, cols).reshape(BLOCK, cols, chan)
            centre = xm[pl.ds(2 + b * BLOCK, BLOCK), :, chan : 2 * chan].astype(F32)
            total = total + centre
            ob[f, pl.ds(b * BLOCK, BLOCK)] = total.astype(BF16)
            if f + 1 < frames:
                for q in range(half):
                    to_blocks(f + 1, b, q, total[:, q * 2 * BLOCK : (q + 1) * 2 * BLOCK])
            return carry

        lax.fori_loop(0, band, last_body, 0)
        if f + 1 < frames:
            pack_and_send(f + 1)
        pltpu.make_async_copy(ob.at[f], out.at[f], out_sem.at[f]).start()

    for f in range(frames):
        pltpu.make_async_copy(ob.at[f], out.at[f], out_sem.at[f]).wait()
    each_side(lambda side: list_copy(side).wait_send())
    each_side(lambda side: feature_copy(side).wait_send())
    for f in range(frames):
        each_side(lambda side: pack_copy(f, side).wait_send())
        each_side(lambda side: halo_copy(f, side).wait_send())


def on_device(group, state, features, row_moves, col_moves, w_merge, w_first, w_second):
    frames, rows, cols, chan = features.shape
    band, across = rows // BLOCK, cols // BLOCK
    blocks = band * across
    slots = blocks // 2
    area = BLOCK * BLOCK
    me = lax.axis_index("rows")

    ids = jnp.arange(blocks, dtype=jnp.int32)
    src_row = jnp.clip(me * band + ids // across + row_moves, 0, band * group - 1)
    src_col = jnp.clip(ids % across + col_moves, 0, across - 1)
    rel = src_row - (me - 1) * band
    where_from = rel // band
    block = (rel % band) * across + src_col
    picks = block
    lists = []
    for side in (0, 1):
        mine = where_from == 2 * side
        earlier = mine[:, None, :] & (ids[None, None, :] < ids[None, :, None])
        rank = jnp.sum(earlier.astype(jnp.int32), axis=-1)
        hit = mine[:, None, :] & (rank[:, None, :] == jnp.arange(slots, dtype=jnp.int32)[None, :, None])
        lists.append(jnp.sum(jnp.where(hit, block[:, None, :], 0), axis=-1))
        picks = jnp.where(mine, blocks + side * slots + rank, picks)
    lists = jnp.pad(jnp.stack(lists), ((0, 0), (0, 8 - frames), (0, 128 - slots)))

    any_spec = pl.BlockSpec(memory_space=pl.ANY)
    copies = 2 + 2 * frames
    scratch = [
        pltpu.VMEM(state.shape, BF16),
        pltpu.VMEM(features.shape, BF16),
        pltpu.VMEM(w_merge.shape, BF16),
        pltpu.VMEM(w_first.shape, BF16),
        pltpu.VMEM(w_second.shape, BF16),
        [pltpu.VMEM((blocks, area, chan), BF16)] * frames,
        [pltpu.VMEM((blocks + 2 * slots, area, chan), BF16)] * frames,
        pltpu.VMEM((frames, 2, slots, area, chan), BF16),
        pltpu.VMEM((frames, rows + 6, cols, 3 * chan), BF16),
        pltpu.VMEM((rows + 6, cols, 3 * chan), BF16),
        pltpu.VMEM((rows + 4, cols, 3 * chan), BF16),
        pltpu.VMEM((rows + 2, cols, 3 * chan), BF16),
        pltpu.VMEM((frames, rows // 2 + 2, cols, 2 * chan), F32),
        pltpu.VMEM((frames, rows, cols, chan), BF16),
        pltpu.VMEM((frames, rows, cols, chan), BF16),
    ] + [pltpu.VMEM((12 * chan, 2 * chan), BF16)] * 4 + [
        pltpu.VMEM((2, 8, 128), jnp.int32),
        pltpu.SMEM((2, 8, 128), jnp.int32),
        pltpu.VMEM((2, frames, 3, cols, chan), BF16),
        pltpu.VMEM((frames, 2, 3, cols, chan), BF16),
        pltpu.SemaphoreType.DMA((5,)),
        pltpu.SemaphoreType.DMA((2,)),
        pltpu.SemaphoreType.DMA((frames,)),
        pltpu.SemaphoreType.DMA((copies, 2)),
        pltpu.SemaphoreType.DMA((copies, 2)),
    ]
    return pl.pallas_call(
        functools.partial(kernel, group),
        out_shape=jax.ShapeDtypeStruct(features.shape, BF16),
        in_specs=[
            pl.BlockSpec(memory_space=pltpu.SMEM),
            pl.BlockSpec(memory_space=pltpu.VMEM),
        ] + [any_spec] * 5,
        out_specs=any_spec,
        scratch_shapes=scratch,
        compiler_params=pltpu.CompilerParams(
            collective_id=0, has_side_effects=True, vmem_limit_bytes=58 * 1024 * 1024
        ),
    )(picks, lists, state, features, w_merge, w_first, w_second)


def solution(mesh):
    blocked = P(("clips", "rows"), None, None)
    framed = P(None, ("clips", "rows"), None, None)
    moves = P(None, ("clips", "rows"))
    return jax.shard_map(
        functools.partial(on_device, mesh.shape["rows"]),
        mesh=mesh,
        in_specs=(blocked, framed, moves, moves, P(), P(), P()),
        out_specs=framed,
        check_vma=False,
    )
```

profile of v0, /device:TPU:1, one launch (start us, length us, event | category | flops | bytes accessed | tf_op | source)
XLA Modules:
  0.0 60.5 jit_solution(13812104143037472852)
XLA Ops:
  0.0 0.7 %broadcast_compare_fusion.1 = (pred[2,64]{1,0:T(4,128)(4,1)S(1)}, s32[2,64]{1,0:T(2,128)S(1)}) fusion(s32[]{:T(128)S(6)} %mul.13, s32[2,64]{1,0:T(2,128)} %param.9, s32[64]{0:T(128)S(1)} %get-tuple-element.14), kind=kLoop, calls=%fused_computation.26 | loop fusion | flops 2432 | bytes 1412 | tf_op jit(solution)/shard_map/eq | solution.py:291
  0.7 0.1 convert_reduce_fusion.1
  0.9 1.3 %select_select_fusion = (s32[2,64]{1,0:T(2,128)}, s32[2,64]{1,0:T(2,128)S(1)}) fusion(pred[2,64]{1,0:T(4,128)(4,1)S(1)} %get-tuple-element.11, s32[2,64]{1,0:T(2,128)S(1)} %get-tuple-element.6, s32[2,64]{1,0:T(2,128)S(1)} %get-tuple-element.5, s32[2,64]{1,0:T(2,128)} %param.10, s32[64]{0:T(128)S(1)} %get-tuple-element.13, s32[]{:T(128)S(6)} %mul.13, ...), kind=kLoop, calls=%fused_computation.19 | loop fusion | flops 2944 | bytes 4228 | tf_op jit(solution)/shard_map/jit(_where)/select_n | solution.py:296
  2.2 0.1 select_reduce_fusion.1
  2.4 0.6 %pad.4.lists = s32[2,8,128]{2,1,0:T(8,128)} pad(s32[2,2,32]{2,1,0:T(2,128)S(1)} %pad_add_fusion, s32[]{:T(128)} %constant.60.clone.1), padding=0_0x0_6x0_96 | pad | bytes 8708 | tf_op jit(solution)/shard_map/jit(_pad)/pad | solution.py:297
  3.0 54.4 %shard_map.73 = bf16[2,32,128,128]{3,2,1,0:T(8,128)(2,1)} custom-call(s32[2,64]{1,0:T(2,128)} %get-tuple-element.9.picks, s32[2,8,128]{2,1,0:T(8,128)} %pad.4.lists, bf16[32,128,128]{2,1,0:T(8,128)(2,1)} %state.1, bf16[2,32,128,128]{3,2,1,0:T(8,128)(2,1)} %features.1, bf16[3,3,256,128]{3,2,1,0:T(8,128)(2,1)} %w_merge.1, bf16[3,3,128,128]{3,2,1,0:T(8,128)(2,1)} %w_first.1, ...), custom_call_target="tpu_custom_call" | custom-call | tf_op jit(solution)/shard_map/pallas_call | solution.py:328
  57.4 3.2 %copy.9 = bf16[2,32,128,128]{3,2,1,0:T(8,128)(2,1)} copy(bf16[2,32,128,128]{3,2,1,0:T(8,128)(2,1)} %shard_map.73) | data formatting | bytes 4194304
  (4 shorter events, 0.0 us)
where the time goes:
time: 60.8 us; the launch traced here: 60.5 us
  Pallas kernels  54.4 us (89%)
  local copies, waits for them, and re-layouts  3.77 us (6%)
  other arithmetic  2.33 us (4%)
    pallas_call x1, Pallas kernels, on_device(): pl.pallas_call(functools.partial(kernel, group), out_shape=jax.ShapeDtype...  54.4 us
    unnamed x1, local copies, waits for them, and re-layouts  3.16 us
    select_n x1, other arithmetic, on_device(): picks = jnp.where(mine, blocks + side * slots + rank, picks)  1.31 us

commit v1 on v0

--- a/solution.py
+++ b/solution.py
@@ -37,11 +37,47 @@
     return jnp.stack([even, odd], axis=1).reshape(2 * count * cols, chan)
 
 
+def make_lists(me, group, band, across, row_moves, col_moves, moved, lists, picks_v):
+    frames, blocks = row_moves.shape
+    slots = lists.shape[1]
+    lanes = moved.shape[2]
+    moved[...] = jnp.zeros_like(moved)
+    moved[0, :frames, :blocks] = row_moves[...]
+    moved[1, :frames, :blocks] = col_moves[...]
+    shape = moved.shape[1:]
+    j = lax.broadcasted_iota(jnp.int32, shape, 1)
+    src_row = jnp.clip(me * band + lax.div(j, across) + moved[0], 0, band * group - 1)
+    src_col = jnp.clip(lax.rem(j, across) + moved[1], 0, across - 1)
+    rel = src_row - (me - 1) * band
+    valid = j < blocks
+    within = jnp.where(rel < band, rel, jnp.where(rel < 2 * band, rel - band, rel - 2 * band))
+    block = within * across + src_col
+    picks = block
+    slot = lax.broadcasted_iota(jnp.int32, (slots, lanes), 0)
+    lane = lax.broadcasted_iota(jnp.int32, (slots, lanes), 1)
+    for side in (0, 1):
+        mine = valid & (rel < band if side == 0 else rel >= 2 * band)
+        total = mine.astype(jnp.int32)
+        step = 1
+        while step < blocks:
+            total = total + jnp.where(j >= step, pltpu.roll(total, step, 1), 0)
+            step *= 2
+        rank = jnp.where(mine, total - 1, -1)
+        picks = jnp.where(mine, blocks + side * slots + rank, picks)
+        wanted = jnp.zeros((slots, lanes), jnp.int32)
+        for f in range(frames):
+            hit = jnp.broadcast_to(rank[f : f + 1], (slots, lanes)) == slot
+            column = jnp.sum(jnp.where(hit, jnp.broadcast_to(block[f : f + 1], (slots, lanes)), 0), axis=1, keepdims=True)
+            wanted = jnp.where(lane == f, column, wanted)
+        lists[side] = wanted
+    picks_v[...] = picks
+
+
 def kernel(
-    group, picks, lists, state, features, w_merge, w_first, w_second, out,
-    st, ft, wm, w1, w2, own, pool, packed, xf, xw, xm, xd, acc, wp, ob,
-    big_f, big_w, big_1, big_2, want_v, want, halo_f, halo_w,
-    load_sem, want_sem, out_sem, send_sem, recv_sem,
+    group, row_moves, col_moves, state, features, w_merge, w_first, w_second, out,
+    st, ft, wm, w1, w2, own, pool, packed, xf, xw, xm, xd, acc, wp,
+    big_f, big_w, big_1, big_2, moved, lists, picks_v, picks, want_v, want, halo_f, halo_w,
+    load_sem, want_sem, send_sem, recv_sem,
 ):
     frames, rows, cols, chan = features.shape
     band, across = rows // BLOCK, cols // BLOCK
@@ -64,6 +100,7 @@
         @pl.when(has[side])
         def _():
             pl.semaphore_signal(barrier, inc=1, device_id={"rows": peer[side]}, device_id_type=MESH)
+    make_lists(me, group, band, across, row_moves, col_moves, moved, lists, picks_v)
     pl.semaphore_wait(barrier, has[0].astype(jnp.int32) + has[1].astype(jnp.int32))
 
     def remote(kind, side, src, dst):
@@ -76,16 +113,16 @@
     def list_copy(side):
         return remote(0, side, lists.at[side], want_v.at[1 - side])
 
-    def feature_copy(side):
+    def feature_copy(f, side):
         edge = pl.ds(0, 3) if side == 0 else pl.ds(rows - 3, 3)
-        return remote(1, side, features.at[:, edge], halo_f.at[1 - side])
+        return remote(1 + f, side, features.at[f, edge], halo_f.at[f, 1 - side])
 
     def pack_copy(f, side):
-        return remote(2 + f, side, packed.at[f, side], pool[f].at[pl.ds(blocks + (1 - side) * slots, slots)])
+        return remote(1 + frames + f, side, packed.at[f, side], pool[f].at[pl.ds(blocks + (1 - side) * slots, slots)])
 
     def halo_copy(f, side):
         edge = pl.ds(0, 3) if side == 0 else pl.ds(rows - 3, 3)
-        return remote(2 + frames + f, side, wp.at[f, edge], halo_w.at[f, 1 - side])
+        return remote(1 + 2 * frames + f, side, wp.at[f, edge], halo_w.at[f, 1 - side])
 
     def each_side(action):
         for side in (0, 1):
@@ -97,7 +134,9 @@
         copy_of(1 - side).wait_recv()
 
     each_side(lambda side: list_copy(side).start())
-    each_side(lambda side: feature_copy(side).start())
+    each_side(lambda side: feature_copy(0, side).start())
+    picks_copy = pltpu.make_async_copy(picks_v, picks, want_sem.at[2])
+    picks_copy.start()
 
     def to_blocks(f, b, q, strip):
         for h in (0, 1):
@@ -127,7 +166,7 @@
         def action(side):
             def body(k, carry):
                 for u in range(4):
-                    packed[f, side, 4 * k + u] = own[f][want[side, f, 4 * k + u]]
+                    packed[f, side, 4 * k + u] = own[f][want[side, 4 * k + u, f]]
                 return carry
             lax.fori_loop(0, slots // 4, body, 0)
             pack_copy(f, side).start()
@@ -171,35 +210,36 @@
     def edge_zero(dst, start, count):
         dst[pl.ds(start, count)] = jnp.zeros((count,) + dst.shape[1:], BF16)
 
-    for f in range(frames):
-        fill_taps(xf.at[f], ft.at[f], 3, rows, 4)
+    pairs = rows // 2
+
+    def feature_conv(f):
+        fill_taps(xf, ft.at[f], 3, rows, 4)
+        for side in (0, 1):
+            @pl.when(has[side])
+            def _():
+                arrived(functools.partial(feature_copy, f), side)
+                edge_rows(xf, halo_f.at[f, side], side)
+
+        def feature_body(i, carry):
+            count = (pairs + 2) // 3
+            acc[pl.ds(i * count, count)] = conv_pairs(xf, i * count, count, big_f).reshape(count, cols, 2 * chan)
+            return carry
+        lax.fori_loop(0, 3, feature_body, 0)
+
     for side in (0, 1):
-        @pl.when(has[side])
-        def _():
-            arrived(feature_copy, side)
-            for f in range(frames):
-                edge_rows(xf.at[f], halo_f.at[side, f], side)
-
         @pl.when(jnp.logical_not(has[side]))
         def _():
-            for f in range(frames):
-                edge_zero(xf.at[f], 0 if side == 0 else rows + 3, 3)
+            edge_zero(xf, 0 if side == 0 else rows + 3, 3)
             edge_zero(xw, 0 if side == 0 else rows + 3, 3)
-
-    pairs = rows // 2
-    for f in range(frames):
-        def feature_body(i, carry):
-            count = (pairs + 2) // 3
-            acc[f, pl.ds(i * count, count)] = conv_pairs(xf.at[f], i * count, count, big_f).reshape(count, cols, 2 * chan)
-            return carry
-        lax.fori_loop(0, 3, feature_body, 0)
+    picks_copy.wait()
 
     def merge_pairs(f, pair, count):
-        total = acc[f, pl.ds(pair, count)].reshape(count * cols, 2 * chan) + conv_pairs(xw, pair, count, big_w)
+        total = acc[pl.ds(pair, count)].reshape(count * cols, 2 * chan) + conv_pairs(xw, pair, count, big_w)
         total = jnp.maximum(total, 0.1 * total)
         put_taps(xm, 2 * pair, unpair(total, count, cols), 2 * count)
 
     for f in range(frames):
+        feature_conv(f)
         each_side(lambda side: arrived(functools.partial(pack_copy, f), side))
 
         def gather_body(i, carry):
@@ -215,6 +255,8 @@
         lax.fori_loop(0, half, gather_body, 0)
         lax.fori_loop((band - 1) * half, band * half, gather_body, 0)
         each_side(lambda side: halo_copy(f, side).start())
+        if f + 1 < frames:
+            each_side(lambda side: feature_copy(f + 1, side).start())
         lax.fori_loop(half, (band - 1) * half, gather_body, 0)
         fill_taps(xw, wp.at[f], 3, rows, 4)
 
@@ -251,7 +293,7 @@
             total = unpair(conv_pairs(xd, b * per, per, big_2), per, cols).reshape(BLOCK, cols, chan)
             centre = xm[pl.ds(2 + b * BLOCK, BLOCK), :, chan : 2 * chan].astype(F32)
             total = total + centre
-            ob[f, pl.ds(b * BLOCK, BLOCK)] = total.astype(BF16)
+            out[f, pl.ds(b * BLOCK, BLOCK)] = total.astype(BF16)
             if f + 1 < frames:
                 for q in range(half):
                     to_blocks(f + 1, b, q, total[:, q * 2 * BLOCK : (q + 1) * 2 * BLOCK])
@@ -260,15 +302,26 @@
         lax.fori_loop(0, band, last_body, 0)
         if f + 1 < frames:
             pack_and_send(f + 1)
-        pltpu.make_async_copy(ob.at[f], out.at[f], out_sem.at[f]).start()
-
+
+    each_side(lambda side: list_copy(side).wait_send())
     for f in range(frames):
-        pltpu.make_async_copy(ob.at[f], out.at[f], out_sem.at[f]).wait()
-    each_side(lambda side: list_copy(side).wait_send())
-    each_side(lambda side: feature_copy(side).wait_send())
-    for f in range(frames):
+        each_side(lambda side: feature_copy(f, side).wait_send())
         each_side(lambda side: pack_copy(f, side).wait_send())
         each_side(lambda side: halo_copy(f, side).wait_send())
+
+
+def deliver(parts, held, out, sem):
+    frames, rows = out.shape[:2]
+    step = rows // parts
+    copies = [
+        pltpu.make_async_copy(held.at[f, pl.ds(i * step, step)], out.at[f, pl.ds(i * step, step)], sem.at[f, i])
+        for f in range(frames)
+        for i in range(parts)
+    ]
+    for copy in copies:
+        copy.start()
+    for copy in copies:
+        copy.wait()
 
 
 def on_device(group, state, features, row_moves, col_moves, w_merge, w_first, w_second):
@@ -277,27 +330,9 @@
     blocks = band * across
     slots = blocks // 2
     area = BLOCK * BLOCK
-    me = lax.axis_index("rows")
-
-    ids = jnp.arange(blocks, dtype=jnp.int32)
-    src_row = jnp.clip(me * band + ids // across + row_moves, 0, band * group - 1)
-    src_col = jnp.clip(ids % across + col_moves, 0, across - 1)
-    rel = src_row - (me - 1) * band
-    where_from = rel // band
-    block = (rel % band) * across + src_col
-    picks = block
-    lists = []
-    for side in (0, 1):
-        mine = where_from == 2 * side
-        earlier = mine[:, None, :] & (ids[None, None, :] < ids[None, :, None])
-        rank = jnp.sum(earlier.astype(jnp.int32), axis=-1)
-        hit = mine[:, None, :] & (rank[:, None, :] == jnp.arange(slots, dtype=jnp.int32)[None, :, None])
-        lists.append(jnp.sum(jnp.where(hit, block[:, None, :], 0), axis=-1))
-        picks = jnp.where(mine, blocks + side * slots + rank, picks)
-    lists = jnp.pad(jnp.stack(lists), ((0, 0), (0, 8 - frames), (0, 128 - slots)))
-
+    lanes = -(-blocks // 128) * 128
     any_spec = pl.BlockSpec(memory_space=pl.ANY)
-    copies = 2 + 2 * frames
+    copies = 1 + 3 * frames
     scratch = [
         pltpu.VMEM(state.shape, BF16),
         pltpu.VMEM(features.shape, BF16),
@@ -307,37 +342,48 @@
         [pltpu.VMEM((blocks, area, chan), BF16)] * frames,
         [pltpu.VMEM((blocks + 2 * slots, area, chan), BF16)] * frames,
         pltpu.VMEM((frames, 2, slots, area, chan), BF16),
-        pltpu.VMEM((frames, rows + 6, cols, 3 * chan), BF16),
+        pltpu.VMEM((rows + 6, cols, 3 * chan), BF16),
         pltpu.VMEM((rows + 6, cols, 3 * chan), BF16),
         pltpu.VMEM((rows + 4, cols, 3 * chan), BF16),
         pltpu.VMEM((rows + 2, cols, 3 * chan), BF16),
-        pltpu.VMEM((frames, rows // 2 + 2, cols, 2 * chan), F32),
-        pltpu.VMEM((frames, rows, cols, chan), BF16),
+        pltpu.VMEM((rows // 2 + 2, cols, 2 * chan), F32),
         pltpu.VMEM((frames, rows, cols, chan), BF16),
     ] + [pltpu.VMEM((12 * chan, 2 * chan), BF16)] * 4 + [
-        pltpu.VMEM((2, 8, 128), jnp.int32),
-        pltpu.SMEM((2, 8, 128), jnp.int32),
-        pltpu.VMEM((2, frames, 3, cols, chan), BF16),
+        pltpu.VMEM((2, 8, lanes), jnp.int32),
+        pltpu.VMEM((2, slots, lanes), jnp.int32),
+        pltpu.VMEM((8, lanes), jnp.int32),
+        pltpu.SMEM((8, lanes), jnp.int32),
+        pltpu.VMEM((2, slots, lanes), jnp.int32),
+        pltpu.SMEM((2, slots, lanes), jnp.int32),
+        pltpu.VMEM((frames, 2, 3, cols, chan), BF16),
         pltpu.VMEM((frames, 2, 3, cols, chan), BF16),
         pltpu.SemaphoreType.DMA((5,)),
-        pltpu.SemaphoreType.DMA((2,)),
-        pltpu.SemaphoreType.DMA((frames,)),
+        pltpu.SemaphoreType.DMA((3,)),
         pltpu.SemaphoreType.DMA((copies, 2)),
         pltpu.SemaphoreType.DMA((copies, 2)),
     ]
-    return pl.pallas_call(
+    held = pl.pallas_call(
         functools.partial(kernel, group),
         out_shape=jax.ShapeDtypeStruct(features.shape, BF16),
         in_specs=[
-            pl.BlockSpec(memory_space=pltpu.SMEM),
             pl.BlockSpec(memory_space=pltpu.VMEM),
-        ] + [any_spec] * 5,
-        out_specs=any_spec,
+            pl.BlockSpec(memory_space=pltpu.VMEM),
+        ] + [pl.BlockSpec(memory_space=pltpu.HBM)] * 5,
+        out_specs=pl.BlockSpec(memory_space=pltpu.VMEM),
         scratch_shapes=scratch,
         compiler_params=pltpu.CompilerParams(
-            collective_id=0, has_side_effects=True, vmem_limit_bytes=58 * 1024 * 1024
+            collective_id=0, has_side_effects=True, vmem_limit_bytes=40 * 1024 * 1024
         ),
-    )(picks, lists, state, features, w_merge, w_first, w_second)
+    )(row_moves, col_moves, state, features, w_merge, w_first, w_second)
+    parts = 2
+    return pl.pallas_call(
+        functools.partial(deliver, parts),
+        out_shape=jax.ShapeDtypeStruct(features.shape, BF16),
+        in_specs=[any_spec],
+        out_specs=any_spec,
+        scratch_shapes=[pltpu.SemaphoreType.DMA((frames, parts))],
+        compiler_params=pltpu.CompilerParams(vmem_limit_bytes=8 * 1024 * 1024),
+    )(held)
 
 
 def solution(mesh):

time: 60.8 us -> 62.6 us (1.030)
  local copies, waits for them, and re-layouts: 3.77 us -> 7.16 us
  other arithmetic: 2.33 us -> 0 us
  Pallas kernels: 54.4 us -> 55.1 us
    unnamed x1 -> x14, local copies, waits for them, and re-layouts: 3.16 us -> 7.16 us
    pallas_call x0 -> x1, Pallas kernels: none -> 1.35 us  [on_device(): pl.pallas_call(functools.partial(deliver, parts), out_shape=jax.ShapeDtyp...]
    select_n x2 -> x0, other arithmetic: 1.31 us -> none  [the longest x1 1.31 us: on_device(): picks = jnp.where(mine, blocks + side * slots + rank, picks)]
    eq x2 -> x0, other arithmetic: 0.7 us -> none  [on_device(): mine = where_from == 2 * side]
where the time goes in v1:
time: 62.6 us; the launch traced here: 62.3 us
  Pallas kernels  55.1 us (88%)
  local copies, waits for them, and re-layouts  7.16 us (11%)
    pallas_call x1, Pallas kernels, on_device(): pl.pallas_call(functools.partial(kernel, group), out_shape=jax.ShapeDtype...  53.8 us
    unnamed x14, local copies, waits for them, and re-layouts  7.16 us
    pallas_call x1, Pallas kernels, on_device(): pl.pallas_call(functools.partial(deliver, parts), out_shape=jax.ShapeDtyp...  1.35 us

profile of v1, /device:TPU:1, one launch (start us, length us, event | category | flops | bytes accessed | tf_op | source)
XLA Modules:
  0.0 62.3 jit_solution(10467006380612660467)
XLA Ops:
  0.0 0.0 copy-start
  0.0 1.6 %copy-done = bf16[2,32,128,128]{3,2,1,0:T(8,128)(2,1)S(1)} copy-done((bf16[2,32,128,128]{3,2,1,0:T(8,128)(2,1)S(1)}, bf16[2,32,128,128]{3,2,1,0:T(8,128)(2,1)}, u32[]{:S(2)}) %copy-start) | copy-done | bytes 2097176
  1.6 0.0 copy-start.1
  1.6 1.2 %copy-done.1 = bf16[32,128,128]{2,1,0:T(8,128)(2,1)S(1)} copy-done((bf16[32,128,128]{2,1,0:T(8,128)(2,1)S(1)}, bf16[32,128,128]{2,1,0:T(8,128)(2,1)}, u32[]{:S(2)}) %copy-start.1) | copy-done | bytes 1048600
  2.8 0.0 copy-start.2
  2.8 1.1 %copy-done.2 = bf16[3,3,256,128]{3,2,1,0:T(8,128)(2,1)S(1)} copy-done((bf16[3,3,256,128]{3,2,1,0:T(8,128)(2,1)S(1)}, bf16[3,3,256,128]{3,2,1,0:T(8,128)(2,1)}, u32[]{:S(2)}) %copy-start.2) | copy-done | bytes 589848
  3.9 0.0 copy-start.3
  3.9 1.0 %copy-done.3 = bf16[3,3,128,128]{3,2,1,0:T(8,128)(2,1)S(1)} copy-done((bf16[3,3,128,128]{3,2,1,0:T(8,128)(2,1)S(1)}, bf16[3,3,128,128]{3,2,1,0:T(8,128)(2,1)}, u32[]{:S(2)}) %copy-start.3) | copy-done | bytes 294936
  4.8 0.0 copy-start.4
  4.8 1.0 %copy-done.4 = bf16[3,3,128,128]{3,2,1,0:T(8,128)(2,1)S(1)} copy-done((bf16[3,3,128,128]{3,2,1,0:T(8,128)(2,1)S(1)}, bf16[3,3,128,128]{3,2,1,0:T(8,128)(2,1)}, u32[]{:S(2)}) %copy-start.4) | copy-done | bytes 294936
  5.8 0.0 copy-start.5
  5.8 0.7 %copy-done.5 = s32[2,64]{1,0:T(2,128)S(1)} copy-done((s32[2,64]{1,0:T(2,128)S(1)}, s32[2,64]{1,0:T(2,128)}, u32[]{:S(2)}) %copy-start.5) | copy-done | bytes 536
  6.5 0.0 copy-start.6
  6.5 0.7 %copy-done.6 = s32[2,64]{1,0:T(2,128)S(1)} copy-done((s32[2,64]{1,0:T(2,128)S(1)}, s32[2,64]{1,0:T(2,128)}, u32[]{:S(2)}) %copy-start.6) | copy-done | bytes 536
  7.2 53.8 %shard_map.73.held = bf16[2,32,128,128]{3,2,1,0:T(8,128)(2,1)S(1)} custom-call(s32[2,64]{1,0:T(2,128)S(1)} %copy-done.5, s32[2,64]{1,0:T(2,128)S(1)} %copy-done.6, bf16[32,128,128]{2,1,0:T(8,128)(2,1)S(1)} %copy-done.1, bf16[2,32,128,128]{3,2,1,0:T(8,128)(2,1)S(1)} %copy-done, bf16[3,3,256,128]{3,2,1,0:T(8,128)(2,1)S(1)} %copy-done.2, ...), custom_call_target="tpu_custom_call" | custom-call | tf_op jit(solution)/shard_map/pallas_call | solution.py:365
  61.0 1.3 %shard_map.74 = bf16[2,32,128,128]{3,2,1,0:T(8,128)(2,1)} custom-call(bf16[2,32,128,128]{3,2,1,0:T(8,128)(2,1)S(1)} %shard_map.73.held), custom_call_target="tpu_custom_call" | custom-call | tf_op jit(solution)/shard_map/pallas_call | solution.py:379
Async XLA Ops:
  0.0 1.6 %copy-start = (bf16[2,32,128,128]{3,2,1,0:T(8,128)(2,1)S(1)}, bf16[2,32,128,128]{3,2,1,0:T(8,128)(2,1)}, u32[]{:S(2)}) copy-start(bf16[2,32,128,128]{3,2,1,0:T(8,128)(2,1)} %features.1) | copy-start | bytes 6291460
  1.6 1.2 %copy-start.1 = (bf16[32,128,128]{2,1,0:T(8,128)(2,1)S(1)}, bf16[32,128,128]{2,1,0:T(8,128)(2,1)}, u32[]{:S(2)}) copy-start(bf16[32,128,128]{2,1,0:T(8,128)(2,1)} %state.1) | copy-start | bytes 3145732
  2.8 1.1 %copy-start.2 = (bf16[3,3,256,128]{3,2,1,0:T(8,128)(2,1)S(1)}, bf16[3,3,256,128]{3,2,1,0:T(8,128)(2,1)}, u32[]{:S(2)}) copy-start(bf16[3,3,256,128]{3,2,1,0:T(8,128)(2,1)} %w_merge.1) | copy-start | bytes 1769476
  3.9 1.0 %copy-start.3 = (bf16[3,3,128,128]{3,2,1,0:T(8,128)(2,1)S(1)}, bf16[3,3,128,128]{3,2,1,0:T(8,128)(2,1)}, u32[]{:S(2)}) copy-start(bf16[3,3,128,128]{3,2,1,0:T(8,128)(2,1)} %w_first.1) | copy-start | bytes 884740
  4.8 1.0 %copy-start.4 = (bf16[3,3,128,128]{3,2,1,0:T(8,128)(2,1)S(1)}, bf16[3,3,128,128]{3,2,1,0:T(8,128)(2,1)}, u32[]{:S(2)}) copy-start(bf16[3,3,128,128]{3,2,1,0:T(8,128)(2,1)} %w_second.1) | copy-start | bytes 884740
  5.8 0.7 %copy-start.5 = (s32[2,64]{1,0:T(2,128)S(1)}, s32[2,64]{1,0:T(2,128)}, u32[]{:S(2)}) copy-start(s32[2,64]{1,0:T(2,128)} %row_moves.1) | copy-start | bytes 1540
  6.5 0.7 %copy-start.6 = (s32[2,64]{1,0:T(2,128)S(1)}, s32[2,64]{1,0:T(2,128)}, u32[]{:S(2)}) copy-start(s32[2,64]{1,0:T(2,128)} %col_moves.1) | copy-start | bytes 1540
